TPU v7x, 32 devices: a whole 2x2x4 slice. The times are simulated.
32 devices in a mesh: tile: 8 (over y, x, core), agent: 4 (over z).
Axes of the slice: x: 2, y: 2, z: 4, core: 2. Of those that a mesh axis runs over, the one named last changes fastest.
Arguments:
- agent_state: float32 [4, 1, 16, 128, 256], P(None, None, None, 'tile', 'agent'), may hold values from 0 to 2
- measured: float32 [1, 16, 8192], P(None, None, ('tile', 'agent')), may hold values from 0 to 12
- bin_index: int32 [16, 128, 256], P(None, 'tile', 'agent'), may hold values from 64 to 446, as said below
- bin_frac: int32 [16, 128, 256], P(None, 'tile', 'agent'), may hold values from 0 to 723, as said below
- patch_offsets: int32 [3], replicated, may hold values from 1 to 15
- agent_weights: float32 [4], replicated, may hold values from 0.5 to 2
- up_weight: bfloat16 [3, 256, 4096], P(None, None, 'agent'), may hold values from -0.375 to 0.375
- down_weight: bfloat16 [3, 4096, 256], P(None, 'agent'), may hold values from -0.09375 to 0.09375
Outputs:
- state_next: float32 [4, 1, 16, 128, 256], P(None, None, None, 'tile', 'agent')
- data_fit: float32 [1, 16, 128, 256], P(None, None, 'tile', 'agent')
Inputs may be any that keep to these rules, and one draw needn't show every extreme that they name: bin_index[a, x, y] = floor(((x - 64) c_a + (y - 128) s_a) / 724) + 256 and bin_frac[a, x, y] is the remainder of that division, for whole numbers c_a, s_a of size at most 724 with c_a * c_a + s_a * s_a close to 524176, one pair an angle. bin_frac is the remainder that belongs to bin_index.
All inputs are finite; a program needn't handle non-finite values.
Results may differ from a plain program's by a relative error of at most 0.0003.
The roundings to bfloat16 on the way count: a program that leaves them out, or rounds other values in their place, can miss the bound.
Values may be sent and summed in bfloat16 or wider, within the bound.
A program may use at most 64 MiB of HBM per device.

v0:
```python
import math

import jax
import jax.numpy as jnp
from jax import lax
from jax.sharding import PartitionSpec as P

PATCH = 16


def extended_2(block, sides, width):
    for axis, dim in sides:
        count = lax.axis_size(axis)
        forward = [(i, i + 1) for i in range(count - 1)]
        forward.append((count - 1, 0))
        backward = [(target, source) for source, target in forward]
        low = lax.ppermute(
            lax.slice_in_dim(block, block.shape[dim] - width, None, axis=dim), axis, forward
        )
        high = lax.ppermute(lax.slice_in_dim(block, 0, width, axis=dim), axis, backward)
        block = jnp.concatenate([low, block, high], axis=dim)
    return block


def make_band(low_rel, weight, offsets):
    near = jnp.where(low_rel[:, None] == offsets[None, :], weight[:, None], 0.0)
    far = jnp.where(low_rel[:, None] + 1 == offsets[None, :], (1.0 - weight)[:, None], 0.0)
    return near + far


def data_agent(volume, bin_index, bin_frac, measured, factor, sino_width):
    angles = bin_index.shape[0]
    planes = volume.shape[0] * volume.shape[1]
    current = volume.reshape(planes, -1)
    bins_each = sino_width // angles
    window = (bin_index.shape[1] + bin_index.shape[2] + 2 + 31) // 32 * 32
    offsets = jnp.arange(window, dtype=jnp.int32)
    lows = bin_index.reshape(angles, -1)
    weight = bin_frac.reshape(angles, -1).astype(jnp.float32) / 724.0
    starts = jnp.minimum(jnp.min(lows, axis=1), bins_each - window)
    target = measured.reshape(planes, -1)
    anchor = jnp.zeros((), jnp.int32)
    highest = lax.Precision.HIGHEST

    def place(piece, start):
        return lax.dynamic_update_slice(
            jnp.zeros((planes, bins_each), jnp.float32), piece, (anchor, start)
        )

    def project(carry, item):
        low_a, weight_a, start = item
        band = make_band(low_a - start, weight_a, offsets)
        return (
            carry,
            jnp.dot(current, band, precision=highest, preferred_element_type=jnp.float32),
        )

    unused, windows = lax.scan(project, jnp.zeros((), jnp.float32), (lows, weight, starts))
    partial_sino = jax.vmap(place, in_axes=(0, 0), out_axes=1)(windows, starts).reshape(planes, -1)
    by_tile = lax.psum_scatter(factor * partial_sino, "tile", scatter_dimension=1, tiled=True)
    owned_bins = lax.psum_scatter(by_tile, "agent", scatter_dimension=1, tiled=True)
    misfit = owned_bins - target
    band_bins = lax.all_gather(misfit, "agent", axis=1, tiled=True)
    all_bins = lax.all_gather(band_bins, "tile", axis=1, tiled=True)
    by_angle = jnp.transpose(all_bins.reshape(planes, angles, bins_each), (1, 0, 2))

    def spread(total, item):
        low_a, weight_a, start, resid = item
        band = make_band(low_a - start, weight_a, offsets)
        picked = lax.dynamic_slice_in_dim(resid, start, window, 1)
        return (
            total + jnp.dot(picked, band.T, precision=highest, preferred_element_type=jnp.float32),
            None,
        )

    back_sum, unused = lax.scan(spread, jnp.zeros_like(current), (lows, weight, starts, by_angle))
    current = current - factor * back_sum
    return current.reshape(volume.shape)


def in_plane(extended, shift, apply_net):
    n_time, n_slice, ext_rows, ext_cols = extended.shape
    row_count = ext_rows - 2 * PATCH
    col_count = ext_cols - 2 * PATCH
    row_blocks = row_count // PATCH + 1
    col_blocks = col_count // PATCH + 1
    region = lax.dynamic_slice(
        extended, (0, 0, shift, shift), (n_time, n_slice, row_count + PATCH, col_count + PATCH)
    )
    patches = region.reshape(n_time, n_slice, row_blocks, PATCH, col_blocks, PATCH)
    patches = patches.transpose(0, 1, 2, 4, 3, 5).reshape(-1, PATCH * PATCH)
    result = apply_net(patches)
    result = result.reshape(n_time, n_slice, row_blocks, col_blocks, PATCH, PATCH)
    result = result.transpose(0, 1, 2, 4, 3, 5).reshape(
        n_time, n_slice, row_count + PATCH, col_count + PATCH
    )
    return lax.dynamic_slice(
        result, (0, 0, PATCH - shift, PATCH - shift), (n_time, n_slice, row_count, col_count)
    )


def along_rows(extended, shift, apply_net):
    n_time, n_slice, ext_rows, ext_cols = extended.shape
    row_count = ext_rows - 2 * PATCH
    col_count = ext_cols - 2 * PATCH
    row_blocks = row_count // PATCH + 1
    region = lax.dynamic_slice(
        extended, (0, 0, shift, PATCH), (n_time, n_slice, row_count + PATCH, col_count)
    )
    patches = region.reshape(n_time, n_slice, row_blocks, PATCH, col_count)
    patches = patches.transpose(0, 2, 4, 1, 3).reshape(-1, n_slice * PATCH)
    result = apply_net(patches)
    result = result.reshape(n_time, row_blocks, col_count, n_slice, PATCH)
    result = result.transpose(0, 3, 1, 4, 2).reshape(n_time, n_slice, row_count + PATCH, col_count)
    return lax.dynamic_slice(
        result, (0, 0, PATCH - shift, 0), (n_time, n_slice, row_count, col_count)
    )


def along_cols(extended, shift, apply_net):
    n_time, n_slice, ext_rows, ext_cols = extended.shape
    row_count = ext_rows - 2 * PATCH
    col_count = ext_cols - 2 * PATCH
    col_blocks = col_count // PATCH + 1
    region = lax.dynamic_slice(
        extended, (0, 0, PATCH, shift), (n_time, n_slice, row_count, col_count + PATCH)
    )
    patches = region.reshape(n_time, n_slice, row_count, col_blocks, PATCH)
    patches = patches.transpose(0, 2, 3, 1, 4).reshape(-1, n_slice * PATCH)
    result = apply_net(patches)
    result = result.reshape(n_time, row_count, col_blocks, n_slice, PATCH)
    result = result.transpose(0, 3, 1, 2, 4).reshape(n_time, n_slice, row_count, col_count + PATCH)
    return lax.dynamic_slice(
        result, (0, 0, 0, PATCH - shift), (n_time, n_slice, row_count, col_count)
    )


def shards(
    agent_state, measured, bin_index, bin_frac, patch_offsets, agent_weights, up_weight, down_weight
):
    row_count = agent_state.shape[3]
    col_count = agent_state.shape[4]
    tile_count = lax.axis_size("tile")
    agent_count = lax.axis_size("agent")
    full_rows = row_count * tile_count
    full_cols = col_count * agent_count
    angles = bin_index.shape[0]
    factor = 1.0 / math.sqrt(angles * (full_rows + full_cols))
    sino_width = measured.shape[2] * tile_count * agent_count
    data_fit = data_agent(agent_state[0], bin_index, bin_frac, measured, factor, sino_width)
    noisy = agent_state[1:].astype(jnp.bfloat16)
    extended = extended_2(noisy, (("tile", 3), ("agent", 4)), PATCH)

    def denoiser(which):

        def apply_net(patches):
            hidden = jax.nn.relu(
                jnp.dot(
                    lax.all_gather(patches, "agent", axis=0, tiled=True),
                    up_weight[which],
                    preferred_element_type=jnp.float32,
                )
            ).astype(jnp.bfloat16)
            terms = jnp.dot(hidden, down_weight[which], preferred_element_type=jnp.float32)
            return lax.psum_scatter(terms, "agent", scatter_dimension=0, tiled=True)

        return apply_net

    first = agent_state[1] - in_plane(extended[0], patch_offsets[0], denoiser(0))
    second = agent_state[2] - along_rows(extended[1], patch_offsets[1], denoiser(1))
    third = agent_state[3] - along_cols(extended[2], patch_offsets[2], denoiser(2))
    answers = jnp.stack([data_fit, first, second, third])
    joining = agent_weights / jnp.sum(agent_weights)
    joined = jnp.sum(joining[:, None, None, None, None] * (2.0 * answers - agent_state), axis=0)
    state_next = agent_state + joined[None] - answers
    return (state_next, data_fit)


def solution(mesh):
    placed = (
        P(None, None, None, "tile", "agent"),
        P(None, None, ("tile", "agent")),
        P(None, "tile", "agent"),
        P(None, "tile", "agent"),
        P(),
        P(),
        P(None, None, "agent"),
        P(None, "agent", None),
    )
    return jax.shard_map(
        shards,
        mesh=mesh,
        in_specs=placed,
        out_specs=(P(None, None, None, "tile", "agent"), P(None, None, "tile", "agent")),
        check_vma=False,
    )
```

profile of v0, /device:TPU:0, one launch (start us, length us, event | category | flops | bytes accessed | tf_op | source)
XLA Modules:
  0.0 359.3 jit_solution(17850936079001085720)
XLA Ops:
  8.7 2.9 collective-permute-start.1
  16.1 33.7 %while.29 = (s32[]{:T(128)}, f32[16,16,96]{2,1,0:T(8,128)S(1)}, s32[16,1024]{1,0:T(8,128)S(1)}, s32[16]{0:T(128)S(1)}, f32[16,1024]{1,0:T(8,128)S(1)}, /*index=5*/f32[16,1024]{1,0:T(8,128)S(1)}, s32[]{:T(128)}) while((s32[]{:T(128)}, f32[16,16,96]{2,1,0:T(8,128)S(1)}, s32[16,1024]{1,0:T(8,128)S(1)}, s32[16]{0:T(128)S(1)}, ...), condition=%wide.region_3.4_spmd.clone.clone, body=%wide.region_2.3_spmd.clone.clone.sunk | while | flops 19368960 | bytes 122985 | solution.py:58
  49.9 107.8 %while.28 = (s32[]{:T(128)}, f32[16,16,512]{2,1,0:T(8,128)S(1)}, s32[16,3]{0,1:T(4,128)S(1)}, f32[16,16,96]{2,1,0:T(8,128)S(1)}, s32[]{:T(128)}, /*index=5*/s32[3]{0:T(128)S(1)}, s32[]{:T(128)}) while((s32[]{:T(128)}, f32[16,16,512]{2,1,0:T(8,128)S(1)}, s32[16,3]{0,1:T(4,128)S(1)}, f32[16,16,96]{2,1,0:T(8,128)S(1)}, s32[]{:T(128)}, ...), condition=%wide.while_cond, body=%wide.while_body.sunk | while | flops 1555 | bytes 30891 | solution.py:46
  50.6 2.6 and_reduce_fusion.2
  53.2 1.9 dynamic-slice_select_fusion.2
  57.4 2.6 and_reduce_fusion.2
  60.0 1.9 dynamic-slice_select_fusion.2
  64.1 2.6 and_reduce_fusion.2
  66.7 1.9 dynamic-slice_select_fusion.2
  70.8 2.6 and_reduce_fusion.2
  73.4 1.9 dynamic-slice_select_fusion.2
  77.6 2.6 and_reduce_fusion.2
  80.2 1.9 dynamic-slice_select_fusion.2
  84.3 2.6 and_reduce_fusion.2
  86.9 1.9 dynamic-slice_select_fusion.2
  91.1 2.6 and_reduce_fusion.2
  93.7 1.9 dynamic-slice_select_fusion.2
  97.8 2.6 and_reduce_fusion.2
  100.4 1.9 dynamic-slice_select_fusion.2
  104.5 2.6 and_reduce_fusion.2
  107.1 1.9 dynamic-slice_select_fusion.2
  111.3 2.6 and_reduce_fusion.2
  113.9 1.9 dynamic-slice_select_fusion.2
  118.0 2.6 and_reduce_fusion.2
  120.6 1.9 dynamic-slice_select_fusion.2
  124.8 2.6 and_reduce_fusion.2
  127.3 1.9 dynamic-slice_select_fusion.2
  131.5 2.6 and_reduce_fusion.2
  134.1 1.9 dynamic-slice_select_fusion.2
  138.2 2.6 and_reduce_fusion.2
  140.8 1.9 dynamic-slice_select_fusion.2
  145.0 2.6 and_reduce_fusion.2
  147.6 1.9 dynamic-slice_select_fusion.2
  151.7 2.6 and_reduce_fusion.2
  154.3 1.9 dynamic-slice_select_fusion.2
  159.4 2.3 collective-permute-start.2
  161.9 2.1 collective-permute-start.3
  166.5 3.0 collective-permute-done.2
  169.9 1.8 collective-permute-done.3
  173.4 13.6 %all_gather.19 = bf16[320,256]{1,0:T(8,128)(2,1)S(1)} all-gather(bf16[80,256]{1,0:T(8,128)(2,1)S(1)} %reshape.226), channel_id=1, replica_groups=mesh['tile'=8,'agent'=4] {'agent'}, dimensions={0}, use_global_device_ids=true | all-gather | bytes 204800 | tf_op jit(solution)/shard_map/all_gather | solution.py:159
  187.1 2.5 fusion.27
  191.9 12.8 %all_gather.18 = bf16[512,256]{0,1:T(8,128)(2,1)S(1)} all-gather(bf16[128,256]{0,1:T(8,128)(2,1)S(1)} %reshape.222), channel_id=1, replica_groups=mesh['tile'=8,'agent'=4] {'agent'}, dimensions={0}, use_global_device_ids=true | all-gather | bytes 327680 | tf_op jit(solution)/shard_map/all_gather | solution.py:159
  204.8 2.8 fusion.24
  217.4 2.2 copy.47
  220.1 14.2 %all_gather.17 = bf16[640,256]{1,0:T(8,128)(2,1)S(1)} all-gather(bf16[160,256]{1,0:T(8,128)(2,1)S(1)} %reshape.218), channel_id=1, replica_groups=mesh['tile'=8,'agent'=4] {'agent'}, dimensions={0}, use_global_device_ids=true | all-gather | bytes 409600 | tf_op jit(solution)/shard_map/all_gather | solution.py:159
  234.4 3.0 fusion.23
  240.0 13.3 %all_gather.15 = f32[16,1024]{1,0:T(8,128)S(1)} all-gather(f32[16,256]{1,0:T(8,128)S(1)} %bitcast_subtract_fusion.3), channel_id=1, replica_groups=mesh['tile'=8,'agent'=4] {'agent'}, dimensions={1}, use_global_device_ids=true | all-gather | bytes 81920 | tf_op jit(solution)/shard_map/all_gather | solution.py:63
  253.3 10.3 %all_gather.16 = f32[16,8192]{1,0:T(8,128)S(1)} all-gather(f32[16,1024]{1,0:T(8,128)S(1)} %all_gather.15), channel_id=1, replica_groups=mesh['tile'=8,'agent'=4] {'tile'}, dimensions={1}, use_global_device_ids=true | all-gather | bytes 589824 | tf_op jit(solution)/shard_map/all_gather | solution.py:64
  263.8 81.0 %while.30 = (s32[]{:T(128)}, f32[16,1024]{1,0:T(8,128)S(1)}, s32[16]{0:T(128)S(1)}, f32[16,16,512]{2,0,1:T(8,128)S(1)}, s32[16,1024]{1,0:T(8,128)S(1)}, /*index=...) while((s32[]{:T(128)}, f32[16,1024]{1,0:T(8,128)S(1)}, ...), condition=%wide.region_8.9_spmd.clone.clone, body=%wide.region_7.8_spmd.clone.clone.sunk | while | flops 19401736 | bytes 198873 | solution.py:76
  267.2 1.7 convolution_add_fusion.2
  272.3 1.7 convolution_add_fusion.2
  277.3 1.7 convolution_add_fusion.2
  282.4 1.7 convolution_add_fusion.2
  287.5 1.7 convolution_add_fusion.2
  292.5 1.7 convolution_add_fusion.2
  297.6 1.7 convolution_add_fusion.2
  302.7 1.7 convolution_add_fusion.2
  307.7 1.7 convolution_add_fusion.2
  312.8 1.7 convolution_add_fusion.2
  317.9 1.7 convolution_add_fusion.2
  322.9 1.7 convolution_add_fusion.2
  333.0 1.7 convolution_add_fusion.2
  343.2 1.7 convolution_add_fusion.2
  348.3 2.3 copy.48
  (328 shorter events, 116.2 us)
Async XLA Ops:
  7.2 197.6 %reduce-scatter.6.cloned.1.call-start = ((), (), s32[]{:S(2)}) async-start(), calls=%async_computation.5 | async-start | bytes 589824 | tf_op jit(solution)/shard_map/reduce_scatter | solution.py:60
  8.2 150.5 %collective-permute-start = (bf16[3,1,16,16,64]{4,3,2,1,0:T(8,128)(2,1)S(1)}, bf16[3,1,16,16,64]{4,3,2,1,0:T(8,128)(2,1)S(1)}, u32[]{:S(2)}, u32[]{:S(2)}) collective-permute-start(bf16[3,1,16,16,64]{4,3,2,1,0:T(8,128)(2,1)S(1)} %slice.131), channel_id=1, source_target_pairs={{0,4},{4,8},{8,12},{12,16},{16,20},{20,24},{24,28},{28,0},{1,5},{5... | collective-permute-start | bytes 294920 | tf_op jit(solution)/shard_map/ppermute | solution.py:17
  8.7 150.0 %collective-permute-start.1 = (bf16[3,1,16,16,64]{4,3,2,1,0:T(8,128)(2,1)S(1)}, bf16[3,1,16,16,64]{4,3,2,1,0:T(8,128)(2,1)S(1)}, u32[]{:S(2)}, u32[]{:S(2)}) collective-permute-start(bf16[3,1,16,16,64]{4,3,2,1,0:T(8,128)(2,1)S(1)} %slice.131), channel_id=1, source_target_pairs={{4,0},{8,4},{12,8},{16,12},{20,16},{24,20},{28,24},{0,28},{5,1},{9... | collective-permute-start | bytes 294920 | tf_op jit(solution)/shard_map/ppermute | solution.py:20
  16.1 33.9 %copy-start.2 = (s32[3]{0:T(128)S(1)}, s32[3]{0:T(128)}, u32[]{:S(2)}) copy-start(s32[3]{0:T(128)} %constant.218) | copy-start | bytes 40
  158.7 78.7 %reduce-scatter.14.cloned.1.call-start = ((), (), s32[]{:S(2)}) async-start(), calls=%async_computation.9 | async-start | bytes 409600 | tf_op jit(solution)/shard_map/reduce_scatter | solution.py:165
  158.9 5.1 %copy-start.3 = (s32[3]{0:T(128)S(1)}, s32[3]{0:T(128)}, u32[]{:S(2)}) copy-start(s32[3]{0:T(128)} %param.16) | copy-start | bytes 40
  159.4 10.2 %collective-permute-start.2 = (bf16[3,1,16,48,16]{3,4,2,1,0:T(8,128)(2,1)S(1)}, bf16[3,1,16,48,16]{3,4,2,1,0:T(8,128)(2,1)S(1)}, u32[]{:S(2)}, u32[]{:S(2)}) collective-permute-start(bf16[3,1,16,48,16]{3,4,2,1,0:T(8,128)(2,1)S(1)} %copy.42), channel_id=1, source_target_pairs={{0,1},{1,2},{2,3},{3,0},{4,5},{5,6},{6,7},{7,4},{8,9},{9,10},{10,1... | collective-permute-start | bytes 221192 | tf_op jit(solution)/shard_map/ppermute | solution.py:17
  161.9 9.8 %collective-permute-start.3 = (bf16[3,1,16,48,16]{3,4,2,1,0:T(8,128)(2,1)S(1)}, bf16[3,1,16,48,16]{3,4,2,1,0:T(8,128)(2,1)S(1)}, u32[]{:S(2)}, u32[]{:S(2)}) collective-permute-start(bf16[3,1,16,48,16]{3,4,2,1,0:T(8,128)(2,1)S(1)} %copy.43), channel_id=1, source_target_pairs={{1,0},{2,1},{3,2},{0,3},{5,4},{6,5},{7,6},{4,7},{9,8},{10,9},{11,1... | collective-permute-start | bytes 221192 | tf_op jit(solution)/shard_map/ppermute | solution.py:20
  189.6 49.4 %reduce-scatter.8.cloned.1.call-start = ((), (), s32[]{:S(2)}) async-start(), calls=%async_computation.6 | async-start | bytes 81920 | tf_op jit(solution)/shard_map/reduce_scatter | solution.py:61
  204.8 10.7 %copy-start.4 = (f32[4]{0:T(128)S(1)}, f32[4]{0:T(128)}, u32[]{:S(2)}) copy-start(f32[4]{0:T(128)} %param.17) | copy-start | bytes 52
  204.8 140.9 %reduce-scatter.12.cloned.1.call-start = ((), (), s32[]{:S(2)}) async-start(), calls=%async_computation.8 | async-start | bytes 655360 | tf_op jit(solution)/shard_map/reduce_scatter | solution.py:165
  207.7 139.3 %reduce-scatter.10.cloned.1.call-start = ((), (), s32[]{:S(2)}) async-start(), calls=%async_computation.7 | async-start | bytes 819200 | tf_op jit(solution)/shard_map/reduce_scatter | solution.py:165
  238.5 0.7 copy-start.1
  350.6 1.1 copy-start
Sparse Core Ops, SparseCore 0:
  158.8 35.1 reduce-scatter.5
  196.4 20.0 reduce-scatter.13
  218.9 17.2 reduce-scatter.7
  238.9 19.7 reduce-scatter.11
  260.8 20.6 reduce-scatter.9
where the time goes:
time: 362 us; the launch traced here: 359 us
  other arithmetic  97.7 us (27%)
  local copies, waits for them, and re-layouts  76.1 us (21%)
  blocking collectives  64.3 us (18%)
  matrix products  49.7 us (14%)
  loops' own time  33 us (9%)
  between operations  25.7 us (7%)
  starting transfers between devices  8.03 us (2%)
  waiting for transfers between devices  4.96 us (1%)
    scatter x32, other arithmetic  71.6 us
    all_gather x3, blocking collectives, apply_net(): lax.all_gather(patches, 'agent', axis=0, tiled=True)  40.7 us
    scatter x48, local copies, waits for them, and re-layouts  36.1 us
    another operation x1, loops' own time, data_agent(): lax.scan(spread, jnp.zeros_like(current), (lows, weight, starts, by_angle))  32.2 us
    dot_general x16, matrix products, spread(): jnp.dot(picked, band.T, precision=highest, preferred_element_type=jnp.flo...  27 us
    dynamic_slice x64, local copies, waits for them, and re-layouts, data_agent(): lax.scan(project, jnp.zeros((), jnp.float32), (lows, weight, starts))  19.2 us
    dot_general x16, matrix products, project(): jnp.dot(current, band, precision=highest, preferred_element_type=jnp.floa...  14.3 us
    all_gather x1, blocking collectives, data_agent(): band_bins = lax.all_gather(misfit, 'agent', axis=1, tiled=True)  13.3 us
  transfers between devices with their start and end apart: 9, of which 2 were waited for; matrix products, arithmetic and copies ran while one was open for 60% of the time, Pallas kernels for 0%

commit v1 on v0

v1 whole, which is shorter than its diff:
```python
import functools
import math

import jax
import jax.numpy as jnp
from jax import lax
from jax.experimental import pallas as pl
from jax.experimental.pallas import tpu as pltpu
from jax.sharding import PartitionSpec as P

PATCH = 16
LANES = 128
DENOM = 724.0


def split_pair(values):
    high = values.astype(jnp.bfloat16)
    low = (values - high.astype(jnp.float32)).astype(jnp.bfloat16)
    return high, low


def interpolation_rows(low_ref, frac_ref, angle, start, window):
    lows = low_ref[pl.ds(angle, 1), :] - start
    near = frac_ref[pl.ds(angle, 1), :].astype(jnp.float32) / DENOM
    far = 1.0 - near
    near_high = near.astype(jnp.bfloat16).astype(jnp.float32)
    far_high = far.astype(jnp.bfloat16).astype(jnp.float32)
    near_low, far_low = near - near_high, far - far_high
    apart = lax.broadcasted_iota(jnp.int32, (window, lows.shape[1]), 0) - lows
    at_near, at_far = apart == 0, apart == 1
    high = jnp.where(at_near, near_high, jnp.where(at_far, far_high, 0.0))
    low = jnp.where(at_near, near_low, jnp.where(at_far, far_low, 0.0))
    return jnp.concatenate([high.astype(jnp.bfloat16), low.astype(jnp.bfloat16)], axis=0)


def project_kernel(factor, window, starts_ref, volume_ref, low_ref, frac_ref, sino_ref):
    angles, planes, bins = sino_ref.shape
    high, low = split_pair(volume_ref[...])
    stacked = jnp.concatenate([high, low], axis=0)

    def step(angle, carry):
        start = starts_ref[angle]
        rows = interpolation_rows(low_ref, frac_ref, angle, start, window)
        out = lax.dot_general(
            stacked, rows, (((1,), (1,)), ((), ())), preferred_element_type=jnp.float32
        )
        out = out[:planes] + out[planes:]
        out = factor * (out[:, :window] + out[:, window:])
        if bins > window:
            out = jnp.concatenate([out, jnp.zeros((planes, bins - window), jnp.float32)], axis=1)
            out = pltpu.roll(out, start, 1)
        sino_ref[angle] = out
        return carry

    lax.fori_loop(0, angles, step, 0)


def spread_kernel(factor, window, starts_ref, misfit_ref, low_ref, frac_ref, volume_ref, out_ref):
    angles, planes, bins = misfit_ref.shape
    out_ref[...] = volume_ref[...]

    def step(angle, carry):
        start = starts_ref[angle]
        rows = interpolation_rows(low_ref, frac_ref, angle, start, window)
        resid = misfit_ref[angle]
        if bins > window:
            resid = pltpu.roll(resid, bins - start, 1)[:, :window]
        high, low = split_pair(resid)
        left = jnp.concatenate([high, low], axis=0)
        left = jnp.concatenate([left, left], axis=1)
        out = jnp.dot(left, rows, preferred_element_type=jnp.float32)
        out_ref[...] -= factor * (out[:planes] + out[planes:])
        return carry

    lax.fori_loop(0, angles, step, 0)


def data_agent(volume, bin_index, bin_frac, measured, factor, sino_width):
    angles = bin_index.shape[0]
    planes = volume.shape[0] * volume.shape[1]
    current = volume.reshape(planes, -1)
    bins = sino_width // angles
    window = -(-(bin_index.shape[1] + bin_index.shape[2] + 2) // LANES) * LANES
    window = min(window, bins)
    lows = bin_index.reshape(angles, -1)
    fracs = bin_frac.reshape(angles, -1)
    corners = bin_index[:, :: bin_index.shape[1] - 1, :: bin_index.shape[2] - 1]
    starts = jnp.minimum(jnp.min(corners, axis=(1, 2)), bins - window)
    whole = pl.BlockSpec(memory_space=pltpu.VMEM)
    scalars = pl.BlockSpec(memory_space=pltpu.SMEM)
    cost = pl.CostEstimate(
        flops=4 * angles * window * current.shape[1] * planes * 2,
        bytes_accessed=3 * current.size * 4,
        transcendentals=0,
    )
    grant = pltpu.CompilerParams(vmem_limit_bytes=48 * 2**20)
    sino = pl.pallas_call(
        functools.partial(project_kernel, factor, window),
        out_shape=jax.ShapeDtypeStruct((angles, planes, bins), jnp.float32),
        in_specs=[scalars, whole, whole, whole],
        out_specs=whole,
        cost_estimate=cost,
        compiler_params=grant,
        name="project",
    )(starts, current, lows, fracs)
    partial_sino = jnp.transpose(sino, (1, 0, 2)).reshape(planes, -1)
    by_tile = lax.psum_scatter(partial_sino, "tile", scatter_dimension=1, tiled=True)
    owned_bins = lax.psum_scatter(by_tile, "agent", scatter_dimension=1, tiled=True)
    misfit = owned_bins - measured.reshape(planes, -1)
    band_bins = lax.all_gather(misfit, "agent", axis=1, tiled=True)
    all_bins = lax.all_gather(band_bins, "tile", axis=1, tiled=True)
    by_angle = jnp.transpose(all_bins.reshape(planes, angles, bins), (1, 0, 2))
    result = pl.pallas_call(
        functools.partial(spread_kernel, factor, window),
        out_shape=jax.ShapeDtypeStruct(current.shape, jnp.float32),
        in_specs=[scalars, whole, whole, whole, whole],
        out_specs=whole,
        cost_estimate=cost,
        compiler_params=grant,
        name="spread",
    )(starts, by_angle, lows, fracs, current)
    return result.reshape(volume.shape)


def roll_by(block, shift, axis):
    head = lax.slice_in_dim(block, 0, PATCH, axis=axis)
    return lax.dynamic_slice_in_dim(
        jnp.concatenate([block, head], axis=axis), shift, block.shape[axis], axis
    )


def roll_back(block, shift, axis):
    tail = lax.slice_in_dim(block, block.shape[axis] - PATCH, None, axis=axis)
    return lax.dynamic_slice_in_dim(
        jnp.concatenate([tail, block], axis=axis), PATCH - shift, block.shape[axis], axis
    )


def denoisers(noisy, offsets, up_weight, down_weight):
    tiles = lax.axis_size("tile")
    ahead = [(i, (i + 1) % tiles) for i in range(tiles)]
    behind = [((i + 1) % tiles, i) for i in range(tiles)]
    count, slices, rows, cols = noisy.shape
    below = lax.ppermute(noisy[:2, :, :PATCH], "tile", behind)
    both = jnp.concatenate([noisy[:2], below], axis=2)
    first = lax.dynamic_slice_in_dim(both[0], offsets[0], rows, 1)
    second = lax.dynamic_slice_in_dim(both[1], offsets[1], rows, 1)
    wide = lax.all_gather(jnp.stack([first, second, noisy[2]]), "agent", axis=3, tiled=True)
    width = wide.shape[3]
    row_blocks, col_blocks = rows // PATCH, width // PATCH

    def net(which, patches):
        hidden = jax.nn.relu(
            jnp.dot(patches, up_weight[which], preferred_element_type=jnp.float32)
        ).astype(jnp.bfloat16)
        return jnp.dot(hidden, down_weight[which], preferred_element_type=jnp.float32)

    patches = roll_by(wide[0], offsets[0], 2)
    patches = patches.reshape(slices, row_blocks, PATCH, col_blocks, PATCH)
    patches = patches.transpose(0, 1, 3, 2, 4).reshape(-1, PATCH * PATCH)
    terms = net(0, patches).reshape(slices, row_blocks, col_blocks, PATCH, PATCH)
    terms = terms.transpose(0, 1, 3, 2, 4).reshape(slices, rows, width)
    out_0 = roll_back(terms, offsets[0], 2)

    patches = wide[1].reshape(slices, row_blocks, PATCH, width)
    patches = patches.transpose(1, 3, 0, 2).reshape(-1, slices * PATCH)
    terms = net(1, patches).reshape(row_blocks, width, slices, PATCH)
    out_1 = terms.transpose(2, 0, 3, 1).reshape(slices, rows, width)

    patches = roll_by(wide[2], offsets[2], 2)
    patches = patches.reshape(slices, rows, col_blocks, PATCH)
    patches = patches.transpose(1, 2, 0, 3).reshape(-1, slices * PATCH)
    terms = net(2, patches).reshape(rows, col_blocks, slices, PATCH)
    terms = terms.transpose(2, 0, 1, 3).reshape(slices, rows, width)
    out_2 = roll_back(terms, offsets[2], 2)

    outs = lax.psum_scatter(
        jnp.stack([out_0, out_1, out_2]), "agent", scatter_dimension=3, tiled=True
    )
    above = lax.ppermute(outs[:2, :, rows - PATCH :], "tile", ahead)
    both = jnp.concatenate([above, outs[:2]], axis=2)
    first = lax.dynamic_slice_in_dim(both[0], PATCH - offsets[0], rows, 1)
    second = lax.dynamic_slice_in_dim(both[1], PATCH - offsets[1], rows, 1)
    return jnp.stack([first, second, outs[2]])


def shards(
    agent_state, measured, bin_index, bin_frac, patch_offsets, agent_weights, up_weight, down_weight
):
    row_count = agent_state.shape[3]
    col_count = agent_state.shape[4]
    tile_count = lax.axis_size("tile")
    agent_count = lax.axis_size("agent")
    full_rows = row_count * tile_count
    full_cols = col_count * agent_count
    angles = bin_index.shape[0]
    factor = 1.0 / math.sqrt(angles * (full_rows + full_cols))
    sino_width = measured.shape[2] * tile_count * agent_count
    data_fit = data_agent(agent_state[0], bin_index, bin_frac, measured, factor, sino_width)
    times, slices = agent_state.shape[1], agent_state.shape[2]
    noisy = agent_state[1:].astype(jnp.bfloat16)
    removed = jnp.stack(
        [denoisers(noisy[:, t], patch_offsets, up_weight, down_weight) for t in range(times)], axis=1
    )
    answers = jnp.concatenate([data_fit[None], agent_state[1:] - removed])
    joining = agent_weights / jnp.sum(agent_weights)
    joined = jnp.sum(joining[:, None, None, None, None] * (2.0 * answers - agent_state), axis=0)
    state_next = agent_state + joined[None] - answers
    return (state_next, data_fit)


def solution(mesh):
    placed = (
        P(None, None, None, "tile", "agent"),
        P(None, None, ("tile", "agent")),
        P(None, "tile", "agent"),
        P(None, "tile", "agent"),
        P(),
        P(),
        P(None, None, "agent"),
        P(None, "agent", None),
    )
    return jax.shard_map(
        shards,
        mesh=mesh,
        in_specs=placed,
        out_specs=(P(None, None, None, "tile", "agent"), P(None, None, "tile", "agent")),
        check_vma=False,
    )
```

time: 362 us -> 189 us (0.52)
  other arithmetic: 97.7 us -> 6.31 us
  matrix products: 49.7 us -> 9.96 us
  loops' own time: 33 us -> 0 us
  local copies, waits for them, and re-layouts: 76.1 us -> 43.3 us
  blocking collectives: 64.3 us -> 77.4 us
  Pallas kernels: 0 us -> 13 us
  starting transfers between devices: 8.03 us -> 3.86 us
    scatter x33 -> x0, other arithmetic: 71.7 us -> none
    dot_general x35 -> x5, matrix products: 49.7 us -> 9.96 us  [the longest x3 6.47 us: net(): jnp.dot(hidden, down_weight[which], preferred_element_type=jnp.float32)]
    scatter x48 -> x0, local copies, waits for them, and re-layouts: 36.1 us -> none
    another operation x3 -> x0, loops' own time: 33 us -> none  [the longest x1 32.2 us: data_agent(): lax.scan(spread, jnp.zeros_like(current), (lows, weight, starts, by_angle))]
    dynamic_slice x85 -> x0, local copies, waits for them, and re-layouts: 21.4 us -> none  [the longest x64 19.2 us: data_agent(): lax.scan(project, jnp.zeros((), jnp.float32), (lows, weight, starts))]
    sub x66 -> x2, other arithmetic: 20.5 us -> 0.77 us  [the longest x1 0.72 us: data_agent(): misfit = owned_bins - measured.reshape(planes, -1)]
    unnamed x13 -> x26, local copies, waits for them, and re-layouts: 0.72 us -> 15.4 us
    all_gather x3 -> x1, blocking collectives: 40.7 us -> 54.2 us  [denoisers(): lax.all_gather(jnp.stack([first, second, noisy[2]]), 'agent', axis=3, til...]
  transfers between devices with their start and end apart: 9 -> 5, of which waited for: 2 -> 1; matrix products, arithmetic and copies ran while one was open for 60% -> 29% of each run, Pallas kernels for 0% -> 7%
where the time goes in v1:
time: 189 us; the launch traced here: 187 us
  blocking collectives  77.4 us (41%)
  local copies, waits for them, and re-layouts  43.3 us (23%)
  between operations  25.9 us (14%)
  Pallas kernels  13 us (7%)
  matrix products  9.96 us (5%)
  waiting for transfers between devices  7.12 us (4%)
  other arithmetic  6.31 us (3%)
  starting transfers between devices  3.86 us (2%)
    all_gather x1, blocking collectives, denoisers(): lax.all_gather(jnp.stack([first, second, noisy[2]]), 'agent', axis=3, til...  54.2 us
    unnamed x26, local copies, waits for them, and re-layouts  15.4 us
    all_gather x1, blocking collectives, data_agent(): band_bins = lax.all_gather(misfit, 'agent', axis=1, tiled=True)  13.4 us
    all_gather x1, blocking collectives, data_agent(): all_bins = lax.all_gather(band_bins, 'tile', axis=1, tiled=True)  9.79 us
    pallas_call x1, Pallas kernels, data_agent(): pl.pallas_call(functools.partial(project_kernel, factor, window), out_sha...  7.03 us
    reduce_scatter x1, waiting for transfers between devices, data_agent(): lax.psum_scatter(by_tile, 'agent', scatter_dimension=1, tiled=True)  7.01 us
    dot_general x3, matrix products, net(): jnp.dot(hidden, down_weight[which], preferred_element_type=jnp.float32)  6.47 us
    pallas_call x1, Pallas kernels, data_agent(): pl.pallas_call(functools.partial(spread_kernel, factor, window), out_shap...  5.98 us
  transfers between devices with their start and end apart: 5, of which 1 were waited for; matrix products, arithmetic and copies ran while one was open for 29% of the time, Pallas kernels for 7%

profile of v1, /device:TPU:0, one launch (start us, length us, event | category | flops | bytes accessed | tf_op | source)
XLA Modules:
  0.0 186.9 jit_solution(6437912195116417945)
XLA Ops:
  7.2 1.0 slice.165
  8.3 3.4 %collective-permute-start = (bf16[2,16,16,64]{3,2,1,0:T(8,128)(2,1)S(1)}, bf16[2,16,16,64]{3,2,1,0:T(8,128)(2,1)}, u32[]{:S(2)}, u32[]{:S(2)}) collective-permute-start(bf16[2,16,16,64]{3,2,1,0:T(8,128)(2,1)S(1)} %slice_bitcast_fusion.5), channel_id=1, source_target_pairs={{4,0},{8,4},{12,8},{16,12},{20,16},{24,20},{28,24},{0,28},{5,1},{9... | collective-permute-start | bytes 196616 | tf_op jit(solution)/shard_map/ppermute | solution.py:144
  11.6 0.9 slice.96
  12.6 1.0 reshape.110.low_ref
  13.6 1.0 slice.95
  14.6 0.1 reshape_squeeze.6.volume_ref
  14.7 1.1 reshape.111.frac_ref
  15.8 0.4 reduce_min.9
  16.2 7.0 %project.1 = f32[16,16,512]{2,1,0:T(8,128)S(1)} custom-call(s32[16]{0:T(128)S(1)} %broadcast_minimum_fusion.starts_ref, f32[16,1024]{1,0:T(8,128)S(1)} %reshape_squeeze.6.volume_ref, s32[16,1024]{1,0:T(8,128)S(1)} %reshape.110.low_ref, s32[16,1024]{1,0:T(8,128)S(1)} %reshape.111.frac_ref), custom_call_target="tpu_custom_call" | custom-call | flops 268435456 | bytes 196608 | tf_op jit(solution)/shard_map/project/pallas_call | solution.py:97
  23.2 0.9 copy.110
  24.2 0.6 fusion.23
  33.4 0.1 slice_bitcast_fusion.4
  33.5 1.0 copy.93
  34.5 1.0 copy.99
  35.5 1.0 copy.95
  37.8 0.9 pad_slice_fusion.2
  38.7 0.9 fusion.21
  39.6 0.6 copy.89
  40.2 54.2 %all_gather.11 = bf16[3,16,16,256]{2,1,0,3:T(8,128)(2,1)S(1)} all-gather(bf16[3,16,16,64]{2,1,0,3:T(8,128)(2,1)S(1)} %copy.89), channel_id=1, replica_groups=mesh['tile'=8,'agent'=4] {'agent'}, dimensions={3}, use_global_device_ids=true | all-gather | bytes 491520 | tf_op jit(solution)/shard_map/all_gather | solution.py:148
  94.4 0.5 slice_bitcast_fusion.1
  95.0 1.5 copy.90
  96.5 0.6 slice.129
  97.1 0.8 copy.96
  98.0 1.0 copy.91
  98.9 1.1 fusion.19
  100.0 0.7 reshape.115
  100.7 0.3 copy.92
  101.0 1.7 reshape.116
  102.7 0.1 copy.97
  102.8 0.2 fusion.18
  103.0 0.7 reshape.120
  103.7 0.7 copy.98
  104.4 1.7 reshape.121
  106.1 1.3 fusion
  107.4 2.3 %convolution_bitcast_fusion.1 = f32[16,1,16,16,16]{4,3,2,0,1:T(8,128)S(1)} fusion(bf16[16,16,1024,1]{2,1,3,0:T(8,128)(2,1)S(1)} %bitcast.135, bf16[16,16,1024,1]{2,1,0,3:T(8,128)(2,1)} %bitcast.132), kind=kOutput, calls=%fused_computation.1 | convolution fusion | flops 134217728 | bytes 1310720 | tf_op jit(solution)/shard_map/dot_general | solution.py:156
  109.8 2.1 %fusion.2 = bf16[256,1024]{1,0:T(8,128)(2,1)} fusion(bf16[256,256]{1,0:T(8,128)(2,1)S(1)} %copy-done.6, bf16[3,256,1024]{2,1,0:T(8,128)(2,1)} %param.14), kind=kOutput, calls=%fused_computation.7 | convolution fusion | flops 134742016 | bytes 1179648 | tf_op jit(solution)/shard_map/dot_general | solution.py:154
  111.9 1.5 reshape.118
  113.5 1.0 slice.130
  114.5 2.5 %convolution_bitcast_fusion = f32[16,16,16,16]{3,2,0,1:T(8,128)S(1)} fusion(bf16[16,16,1024,1]{2,1,3,0:T(8,128)(2,1)} %bitcast.134, bf16[16,16,1024,1]{2,1,0,3:T(8,128)(2,1)} %bitcast.131), kind=kOutput, calls=%fused_computation | convolution fusion | flops 134217728 | bytes 1310720 | tf_op jit(solution)/shard_map/dot_general | solution.py:156
  116.9 1.5 reshape.122
  118.5 1.2 copy.100
  119.7 0.8 copy.106
  120.6 0.4 fusion.17
  121.0 0.2 fusion.15
  121.2 1.7 convolution_bitcast_fusion.2
  123.1 5.1 %copy.104 = f32[3,16,16,256]{2,1,0,3:T(8,128)} copy(f32[3,16,16,256]{3,2,1,0:T(8,128)S(1)} %pad_maximum_fusion) | data formatting | bytes 1572864
  128.2 5.7 %reshape.129 = f32[256,768]{1,0:T(8,128)} reshape(f32[256,3,16,16]{3,2,1,0:T(8,128)} %bitcast.123) | data formatting | bytes 1572864
  135.8 0.6 reduce_sum.18
  136.4 0.6 broadcast_divide_fusion
  137.0 7.0 %reduce-scatter.8.cloned.1.call-done = f32[16,256]{1,0:T(8,128)} async-done(((f32[16,1024]{1,0:T(8,128)}), f32[16,256]{1,0:T(8,128)}) %reduce-scatter.8.cloned.1.call-update) | async-done | bytes 16400 | tf_op jit(solution)/shard_map/reduce_scatter | solution.py:108
  144.1 0.7 bitcast_subtract_fusion
  144.8 13.4 %all_gather.9 = f32[16,1024]{1,0:T(8,128)S(1)} all-gather(f32[16,256]{1,0:T(8,128)S(1)} %bitcast_subtract_fusion), channel_id=1, replica_groups=mesh['tile'=8,'agent'=4] {'agent'}, dimensions={1}, use_global_device_ids=true | all-gather | bytes 81920 | tf_op jit(solution)/shard_map/all_gather | solution.py:110
  158.2 9.8 %all_gather.10 = f32[16,8192]{1,0:T(8,128)S(1)} all-gather(f32[16,1024]{1,0:T(8,128)S(1)} %all_gather.9), channel_id=1, replica_groups=mesh['tile'=8,'agent'=4] {'tile'}, dimensions={1}, use_global_device_ids=true | all-gather | bytes 589824 | tf_op jit(solution)/shard_map/all_gather | solution.py:111
  168.0 1.4 reshape.130
  169.5 0.1 slice.135
  169.6 1.4 copy.107
  171.0 0.4 collective-permute-start.1
  171.4 6.0 %spread.1 = f32[16,1024]{1,0:T(8,128)S(1)} custom-call(s32[16]{0:T(128)S(1)} %broadcast_minimum_fusion.starts_ref, f32[16,16,512]{2,1,0:T(8,128)S(1)} %bitcast.121, s32[16,1024]{1,0:T(8,128)S(1)} %reshape.110.low_ref, s32[16,1024]{1,0:T(8,128)S(1)} %reshape.111.frac_ref, f32[16,1024]{1,0:T(8,128)S(1)} %reshape_squeeze.6.volume_ref), custom_call_target="tpu_custom_call" | custom-call | flops 268435456 | bytes 196608 | tf_op jit(solution)/shard_map/spread/pallas_call | solution.py:113
  177.4 0.1 concatenate.31
  177.5 0.7 reshape.123
  178.3 0.3 copy.108
  178.7 0.6 copy-done
  179.3 0.1 multiply_reduce_fusion
  179.5 0.9 add_subtract_fusion
  (44 shorter events, 0.8 us)
Async XLA Ops:
  7.2 115.8 %reduce-scatter.6.cloned.1.call-start = ((), (), s32[]{:S(2)}) async-start(), calls=%async_computation.3 | async-start | bytes 589824 | tf_op jit(solution)/shard_map/reduce_scatter | solution.py:107
  8.3 29.6 %collective-permute-start = (bf16[2,16,16,64]{3,2,1,0:T(8,128)(2,1)S(1)}, bf16[2,16,16,64]{3,2,1,0:T(8,128)(2,1)}, u32[]{:S(2)}, u32[]{:S(2)}) collective-permute-start(bf16[2,16,16,64]{3,2,1,0:T(8,128)(2,1)S(1)} %slice_bitcast_fusion.5), channel_id=1, source_target_pairs={{4,0},{8,4},{12,8},{16,12},{20,16},{24,20},{28,24},{0,28},{5,1},{9... | collective-permute-start | bytes 196616 | tf_op jit(solution)/shard_map/ppermute | solution.py:144
  12.6 11.6 %copy-start.8 = (s32[3]{0:T(128)S(1)}, s32[3]{0:T(128)}, u32[]{:S(2)}) copy-start(s32[3]{0:T(128)} %param.12) | copy-start | bytes 40
  14.6 18.8 %copy-start.3 = (bf16[3,1024,256]{2,1,0:T(8,128)(2,1)S(1)}, bf16[3,1024,256]{2,1,0:T(8,128)(2,1)}, u32[]{:S(2)}) copy-start(bf16[3,1024,256]{2,1,0:T(8,128)(2,1)} %param.15) | copy-start | bytes 4718596
  24.1 119.9 %reduce-scatter.8.cloned.1.call-start = ((), (), s32[]{:S(2)}) async-start(), calls=%async_computation.4 | async-start | bytes 81920 | tf_op jit(solution)/shard_map/reduce_scatter | solution.py:108
  103.7 2.4 %copy-start.5 = (bf16[256,256]{1,0:T(8,128)(2,1)S(1)}, bf16[256,256]{1,0:T(8,128)(2,1)}, u32[]{:S(2)}) copy-start(bf16[256,256]{1,0:T(8,128)(2,1)} %reshape.116) | copy-start | bytes 393220
  107.4 2.3 %copy-start.6 = (bf16[256,256]{1,0:T(8,128)(2,1)S(1)}, bf16[256,256]{1,0:T(8,128)(2,1)}, u32[]{:S(2)}) copy-start(bf16[256,256]{1,0:T(8,128)(2,1)} %reshape.121) | copy-start | bytes 393220
  118.5 2.1 %copy-start.2 = (f32[16,16,256]{2,1,0:T(8,128)S(1)}, f32[16,16,256]{2,1,0:T(8,128)}, u32[]{:S(2)}) copy-start(f32[16,16,256]{2,1,0:T(8,128)} %reshape.118) | copy-start | bytes 786436
  118.5 2.7 %copy-start.4 = (bf16[256,1024]{1,0:T(8,128)(2,1)S(1)}, bf16[256,1024]{1,0:T(8,128)(2,1)}, u32[]{:S(2)}) copy-start(bf16[256,1024]{1,0:T(8,128)(2,1)} %copy.95) | copy-start | bytes 1572868
  123.0 45.1 %reduce-scatter.10.cloned.1.call-start = ((), (), s32[]{:S(2)}) async-start(), calls=%async_computation.5 | async-start | bytes 983040
  128.2 7.6 %copy-start.9 = (f32[4]{0:T(128)S(1)}, f32[4]{0:T(128)}, u32[]{:S(2)}) copy-start(f32[4]{0:T(128)} %param.13) | copy-start | bytes 52
  128.2 15.9 %copy-start.7 = (f32[1,16,256]{2,1,0:T(8,128)S(1)}, f32[1,16,256]{2,1,0:T(8,128)}, u32[]{:S(2)}) copy-start(f32[1,16,256]{2,1,0:T(8,128)} %param.9) | copy-start | bytes 49156
  171.0 7.5 %copy-start.1 = (f32[2,16,16,64]{3,2,1,0:T(8,128)S(1)}, f32[2,16,16,64]{3,2,1,0:T(8,128)}, u32[]{:S(2)}) copy-start(f32[2,16,16,64]{3,2,1,0:T(8,128)} %copy.107) | copy-start | bytes 393220
  171.0 7.5 %collective-permute-start.1 = (f32[2,16,16,64]{3,2,1,0:T(8,128)}, f32[2,16,16,64]{3,2,1,0:T(8,128)S(1)}, u32[]{:S(2)}, u32[]{:S(2)}) collective-permute-start(f32[2,16,16,64]{3,2,1,0:T(8,128)} %copy.107), channel_id=1, source_target_pairs={{0,4},{4,8},{8,12},{12,16},{16,20},{20,24},{24,28},{28,0},{1,5},{5... | collective-permute-start | bytes 393224 | tf_op jit(solution)/shard_map/ppermute | solution.py:180
  178.2 1.0 copy-start
Sparse Core Ops, SparseCore 0:
  24.2 33.6 reduce-scatter.5
  123.1 20.9 reduce-scatter.7
  146.4 21.6 reduce-scatter.9
